TPU v7x, 32 devices: a whole 2x2x4 slice. The times are simulated.
32 devices in a mesh: dp: 16 (over z, y, x), tensor: 2 (over core).
Axes of the slice: x: 2, y: 2, z: 4, core: 2. Of those that a mesh axis runs over, the one named last changes fastest.
Arguments:
- tokens: float32 [16384, 768], P(('dp', 'tensor')), may hold values from -6 to 6
- offsets: int32 [16, 16], P('dp'), may hold values from 0 to 1024, as said below
- w_qkv: bfloat16 [768, 3, 768], P('dp', None, 'tensor'), may hold values from -0.21875 to 0.21875
- w_attn_out: bfloat16 [768, 768], P('tensor', 'dp'), may hold values from -1.75 to 1.75
- w_in: bfloat16 [768, 2, 1152], P('dp', None, 'tensor'), may hold values from -0.21875 to 0.21875
- w_mlp_out: bfloat16 [1152, 768], P('tensor', 'dp'), may hold values from -0.1875 to 0.1875
- gain_attn: bfloat16 [768], P('dp'), may hold values from 0.099609375 to 1.8984375
- gain_mlp: bfloat16 [768], P('dp'), may hold values from 0.099609375 to 1.8984375
- cotangent: float32 [16384, 768], P(('dp', 'tensor')), may hold values from -6 to 6
Outputs:
- outputs: float32 [16384, 768], P(('dp', 'tensor'))
- grad_tokens: float32 [16384, 768], P(('dp', 'tensor'))
- grad_w_qkv: float32 [768, 3, 768], P('dp', None, 'tensor')
- grad_w_attn_out: float32 [768, 768], P('tensor', 'dp')
- grad_w_in: float32 [768, 2, 1152], P('dp', None, 'tensor')
- grad_w_mlp_out: float32 [1152, 768], P('tensor', 'dp')
- grad_gain_attn: float32 [768], P('dp')
- grad_gain_mlp: float32 [768], P('dp')
Inputs may be any that keep to these rules, and one draw needn't show every extreme that they name: `offsets`: each row holds the first tokens of 16 sequences of one group of 1024 tokens, rising from 0 and never falling (equal entries are empty sequences); a sequence ends where the next begins, the last at 1024. No sequence has more than 512 tokens; in every row one has exactly 512 and holds the group's tokens 512 - 1 and 512.
All inputs are finite; a program needn't handle non-finite values.
Results may differ from a plain program's by a relative error of at most 0.018.
Values may be sent and summed in bfloat16 or wider, within the bound.
A program may use at most 128 MiB of HBM per device.

v0:
```python
import math
import jax
import jax.numpy as jnp
from jax import lax
from jax.sharding import PartitionSpec as P

HEAD_DIM = 64
EPSILON = 1e-05
ROPE_BASE = 160000.0
NEGATIVE = -1e30


def seq_starts(offset_row, count_rows):
    position = jnp.arange(count_rows, dtype=jnp.int32)
    before = offset_row[None, :] <= position[:, None]
    return jnp.max(jnp.where(before, offset_row[None, :], 0), axis=1)


def rope_tables(starts):
    count_rows = starts.shape[0]
    position = jnp.arange(count_rows, dtype=jnp.int32) - starts
    half_dim = HEAD_DIM // 2
    inverse = jnp.power(
        jnp.float32(ROPE_BASE), -2.0 * jnp.arange(half_dim, dtype=jnp.float32) / HEAD_DIM
    )
    angles = position.astype(jnp.float32)[:, None] * inverse[None, :]
    return (jnp.cos(angles), jnp.sin(angles))


def rotate(head_rows, cosine_tab, sine_tab):
    half_dim = HEAD_DIM // 2
    first_half = head_rows[..., :half_dim]
    second = head_rows[..., half_dim:]
    cosine_b = cosine_tab[:, None, :]
    sine_b = sine_tab[:, None, :]
    return jnp.concatenate(
        [first_half * cosine_b - second * sine_b, second * cosine_b + first_half * sine_b], axis=-1
    )


def rotate_back(head_grads, cosine_tab, sine_tab):
    half_dim = HEAD_DIM // 2
    first_half = head_grads[..., :half_dim]
    second = head_grads[..., half_dim:]
    cosine_b = cosine_tab[:, None, :]
    sine_b = sine_tab[:, None, :]
    return jnp.concatenate(
        [first_half * cosine_b + second * sine_b, second * cosine_b - first_half * sine_b], axis=-1
    )


def layer_norm(inputs_v, gain_v):
    centre = inputs_v - jnp.mean(inputs_v, axis=-1, keepdims=True)
    spread = jnp.mean(centre * centre, axis=-1, keepdims=True)
    return centre * lax.rsqrt(spread + EPSILON) * gain_v


def exact_gelu(gate_in):
    return jax.nn.gelu(gate_in, approximate=False)


def fetch_attention(w_qkv, w_attn_out, gain_attn):
    return (
        lax.all_gather(w_qkv, "dp", axis=0, tiled=True),
        lax.all_gather(w_attn_out, "dp", axis=1, tiled=True),
        lax.all_gather(gain_attn, "dp", axis=0, tiled=True),
    )


def fetch_attention_again(w_qkv, w_attn_out, gain_attn):
    return (
        lax.all_gather(w_qkv, "dp", axis=0, tiled=True),
        lax.all_gather(w_attn_out, "dp", axis=1, tiled=True),
        lax.all_gather(gain_attn, "dp", axis=0, tiled=True),
    )


def fetch_mlp(w_in, w_mlp_out, gain_mlp):
    return (
        lax.all_gather(w_in, "dp", axis=0, tiled=True),
        lax.all_gather(w_mlp_out, "dp", axis=1, tiled=True),
        lax.all_gather(gain_mlp, "dp", axis=0, tiled=True),
    )


def fetch_mlp_again(w_in, w_mlp_out, gain_mlp):
    return (
        lax.all_gather(w_in, "dp", axis=0, tiled=True),
        lax.all_gather(w_mlp_out, "dp", axis=1, tiled=True),
        lax.all_gather(gain_mlp, "dp", axis=0, tiled=True),
    )


def spread_rows(local_rows):
    return lax.all_gather(local_rows, "tensor", axis=0, tiled=True)


def spread_grads(local_rows):
    return lax.all_gather(local_rows, "tensor", axis=0, tiled=True)


def collect_rows(inputs_all, weight_full, rows_here):

    def term_of(row_start, row_count):
        return jnp.dot(inputs_all, weight_full, preferred_element_type=jnp.float32)

    return lax.psum_scatter(
        term_of(jnp.int32(0), rows_here * lax.axis_size("tensor")).astype(jnp.bfloat16),
        "tensor",
        scatter_dimension=0,
        tiled=True,
    ).astype(jnp.float32)


def collect_grads(grads_all, weight_full, rows_here):

    def term_of(row_start, row_count):
        return jnp.einsum("tsk,dsk->td", grads_all, weight_full, preferred_element_type=jnp.float32)

    return lax.psum_scatter(
        term_of(jnp.int32(0), rows_here * lax.axis_size("tensor")).astype(jnp.bfloat16),
        "tensor",
        scatter_dimension=0,
        tiled=True,
    ).astype(jnp.float32)


def block_scores(query_block, start_block, key_rows, starts, scale_factor):
    raw_scores = (
        jnp.einsum("qhe,khe->hqk", query_block, key_rows, preferred_element_type=jnp.float32)
        * scale_factor
    )
    same_seq = start_block[:, None] == starts[None, :]
    return jnp.where(same_seq[None], raw_scores, NEGATIVE)


def attention_forward(queries, key_rows, values, starts, scale_factor):
    group_rows, heads_here, head_dim = queries.shape
    block_rows = min(512, group_rows)
    block_count = group_rows // block_rows

    def one_block(block_in):
        query_block, start_block = block_in
        masked = block_scores(query_block, start_block, key_rows, starts, scale_factor)
        row_max = jnp.max(masked, axis=-1, keepdims=True)
        exp_terms = jnp.exp(masked - row_max)
        row_total = jnp.sum(exp_terms, axis=-1, keepdims=True)
        softmax_w = exp_terms / row_total
        mixed_out = jnp.einsum(
            "hqk,khe->qhe",
            softmax_w.astype(jnp.bfloat16),
            values,
            preferred_element_type=jnp.float32,
        )
        return (mixed_out, (row_max + jnp.log(row_total))[..., 0])

    mixed_all, lse_stack = lax.map(
        one_block,
        (
            queries.reshape(block_count, block_rows, heads_here, head_dim),
            starts.reshape(block_count, block_rows),
        ),
    )
    return (mixed_all.reshape(group_rows, heads_here, head_dim), lse_stack)


def attention_backward(queries, key_rows, values, starts, lse_stack, grad_out, scale_factor):
    group_rows, heads_here, head_dim = queries.shape
    block_rows = min(512, group_rows)
    block_count = group_rows // block_rows

    def one_block(carry_in, block_in):
        grad_keys, grad_values = carry_in
        query_block, start_block, lse_block, grad_block = block_in
        masked = block_scores(query_block, start_block, key_rows, starts, scale_factor)
        softmax_w = jnp.exp(masked - lse_block[..., None])
        grad_values = grad_values + jnp.einsum(
            "hqk,qhe->khe",
            softmax_w.astype(jnp.bfloat16),
            grad_block,
            preferred_element_type=jnp.float32,
        )
        grad_probs = jnp.einsum(
            "qhe,khe->hqk", grad_block, values, preferred_element_type=jnp.float32
        )
        grad_scores = softmax_w * (
            grad_probs - jnp.sum(softmax_w * grad_probs, axis=-1, keepdims=True)
        )
        rounded = grad_scores.astype(jnp.bfloat16)
        grad_query = (
            jnp.einsum("hqk,khe->qhe", rounded, key_rows, preferred_element_type=jnp.float32)
            * scale_factor
        )
        grad_keys = (
            grad_keys
            + jnp.einsum("hqk,qhe->khe", rounded, query_block, preferred_element_type=jnp.float32)
            * scale_factor
        )
        return ((grad_keys, grad_values), grad_query)

    zero_grads = jnp.zeros((group_rows, heads_here, head_dim), jnp.float32)
    block_inputs = (
        queries.reshape(block_count, block_rows, heads_here, head_dim),
        starts.reshape(block_count, block_rows),
        lse_stack,
        grad_out.reshape(block_count, block_rows, heads_here, head_dim),
    )
    (grad_keys, grad_values), grad_queries = lax.scan(
        one_block, (zero_grads, zero_grads), block_inputs
    )
    return (grad_queries.reshape(group_rows, heads_here, head_dim), grad_keys, grad_values)


def shards(tokens, offsets, w_qkv, w_attn_out, w_in, w_mlp_out, gain_attn, gain_mlp, cotangent):
    rows_here = tokens.shape[0]
    group_rows = rows_here * lax.axis_size("tensor")
    scale_factor = 1.0 / math.sqrt(HEAD_DIM)
    starts = seq_starts(offsets[0], group_rows)
    cosine_tab, sine_tab = rope_tables(starts)
    qkv_full, attn_out_full, gain_one_low = fetch_attention(w_qkv, w_attn_out, gain_attn)
    gain_one = gain_one_low.astype(jnp.float32)
    normed_all = spread_rows(layer_norm(tokens, gain_one).astype(jnp.bfloat16))
    projected = jnp.einsum("td,dsk->tsk", normed_all, qkv_full, preferred_element_type=jnp.float32)
    width_here = projected.shape[2]
    heads_here = width_here // HEAD_DIM
    split_heads = projected.reshape(group_rows, 3, heads_here, HEAD_DIM)
    queries = rotate(split_heads[:, 0], cosine_tab, sine_tab).astype(jnp.bfloat16)
    key_rows = rotate(split_heads[:, 1], cosine_tab, sine_tab).astype(jnp.bfloat16)
    values = split_heads[:, 2].astype(jnp.bfloat16)
    mixed_all, lse_stack = attention_forward(queries, key_rows, values, starts, scale_factor)
    context = mixed_all.reshape(group_rows, width_here).astype(jnp.bfloat16)
    attended = collect_rows(context, attn_out_full, rows_here)
    hidden = tokens + attended
    mlp_in_full, mlp_out_full, gain_two_low = fetch_mlp(w_in, w_mlp_out, gain_mlp)
    gain_two = gain_two_low.astype(jnp.float32)
    mlp_normed = layer_norm(hidden, gain_two).astype(jnp.bfloat16)
    mlp_in_use, mlp_out_use = (mlp_in_full, mlp_out_full)
    mlp_rows = spread_rows(mlp_normed)
    gate_up = jnp.einsum("td,dsf->tsf", mlp_rows, mlp_in_use, preferred_element_type=jnp.float32)
    gate_part = gate_up[:, 0]
    up_part = gate_up[:, 1]
    activated = exact_gelu(gate_part)
    product_rows = (activated * up_part).astype(jnp.bfloat16)
    branch = collect_rows(product_rows, mlp_out_use, rows_here)
    outputs = hidden + branch
    mlp_in_back, mlp_out_back, gain_two_again = fetch_mlp_again(w_in, w_mlp_out, gain_mlp)
    gain_two_back = gain_two_again.astype(jnp.float32)
    grad_rows = spread_grads(cotangent.astype(jnp.bfloat16))
    grad_mlp_out = jnp.einsum(
        "tf,td->fd", product_rows, grad_rows, preferred_element_type=jnp.float32
    )
    grad_product = jnp.einsum(
        "td,fd->tf", grad_rows, mlp_out_back, preferred_element_type=jnp.float32
    )
    unused_out, gelu_pull = jax.vjp(exact_gelu, gate_part)
    grad_gate = gelu_pull(grad_product * up_part)[0]
    grad_up = grad_product * activated
    grad_gate_up = jnp.stack([grad_gate, grad_up], axis=1).astype(jnp.bfloat16)
    grad_mlp_in = jnp.einsum(
        "td,tsf->dsf", mlp_rows, grad_gate_up, preferred_element_type=jnp.float32
    )
    grad_normed_two = collect_grads(grad_gate_up, mlp_in_back, rows_here)
    unused_two, norm_pull_two = jax.vjp(layer_norm, hidden, gain_two_back)
    grad_hidden_norm, grad_gain_two = norm_pull_two(grad_normed_two)
    grad_hidden = cotangent + grad_hidden_norm
    mlp_sums = (
        lax.psum_scatter(grad_mlp_in, "dp", scatter_dimension=0, tiled=True),
        lax.psum_scatter(grad_mlp_out, "dp", scatter_dimension=1, tiled=True),
        lax.psum_scatter(grad_gain_two, "dp", scatter_dimension=0, tiled=True),
    )
    qkv_back, attn_out_back, gain_one_again = fetch_attention_again(w_qkv, w_attn_out, gain_attn)
    gain_one_back = gain_one_again.astype(jnp.float32)
    grad_hidden_rows = spread_grads(grad_hidden.astype(jnp.bfloat16))
    grad_attn_out = jnp.einsum(
        "te,td->ed", context, grad_hidden_rows, preferred_element_type=jnp.float32
    )
    grad_context = jnp.einsum(
        "td,ed->te", grad_hidden_rows, attn_out_back, preferred_element_type=jnp.float32
    ).astype(jnp.bfloat16)
    grad_queries, grad_keys, grad_values = attention_backward(
        queries,
        key_rows,
        values,
        starts,
        lse_stack,
        grad_context.reshape(group_rows, heads_here, HEAD_DIM),
        scale_factor,
    )
    grad_projected = jnp.stack(
        [
            rotate_back(grad_queries, cosine_tab, sine_tab),
            rotate_back(grad_keys, cosine_tab, sine_tab),
            grad_values,
        ],
        axis=1,
    )
    grad_projected = grad_projected.reshape(group_rows, 3, width_here).astype(jnp.bfloat16)
    grad_qkv = jnp.einsum(
        "td,tsk->dsk", normed_all, grad_projected, preferred_element_type=jnp.float32
    )
    grad_normed_one = collect_grads(grad_projected, qkv_back, rows_here)
    unused_one, norm_pull_one = jax.vjp(layer_norm, tokens, gain_one_back)
    grad_tokens_norm, grad_gain_one = norm_pull_one(grad_normed_one)
    grad_tokens = grad_hidden + grad_tokens_norm
    attn_sums = (
        lax.psum_scatter(grad_qkv, "dp", scatter_dimension=0, tiled=True),
        lax.psum_scatter(grad_attn_out, "dp", scatter_dimension=1, tiled=True),
        lax.psum_scatter(grad_gain_one, "dp", scatter_dimension=0, tiled=True),
    )
    shard_mlp_in, shard_mlp_out, shard_gain_two = mlp_sums
    shard_qkv, shard_attn_out, shard_gain_one = attn_sums
    gain_one_total, gain_two_total = lax.psum((shard_gain_one, shard_gain_two), "tensor")
    return (
        outputs,
        grad_tokens,
        shard_qkv,
        shard_attn_out,
        shard_mlp_in,
        shard_mlp_out,
        gain_one_total,
        gain_two_total,
    )


def solution(mesh):
    in_specs = (
        P(("dp", "tensor"), None),
        P("dp", None),
        P("dp", None, "tensor"),
        P("tensor", "dp"),
        P("dp", None, "tensor"),
        P("tensor", "dp"),
        P("dp"),
        P("dp"),
        P(("dp", "tensor"), None),
    )
    out_specs = (
        P(("dp", "tensor"), None),
        P(("dp", "tensor"), None),
        P("dp", None, "tensor"),
        P("tensor", "dp"),
        P("dp", None, "tensor"),
        P("tensor", "dp"),
        P("dp"),
        P("dp"),
    )
    return jax.shard_map(shards, mesh=mesh, in_specs=in_specs, out_specs=out_specs, check_vma=False)
```

profile of v0, /device:TPU:0, one launch (start us, length us, event | category | flops | bytes accessed | tf_op | source)
XLA Modules:
  0.0 875.3 jit_solution(12923273058877242758)
XLA Ops:
  7.3 1.7 reduce_sum.107
  11.2 43.5 %all-reduce.6 = (bf16[768]{0:T(1024)(128)(2,1)S(1)}, bf16[768]{0:T(1024)(128)(2,1)S(1)}) all-reduce(bf16[768]{0:T(1024)(128)(2,1)S(1)} %dynamic-update-slice, bf16[768]{0:T(1024)(128)(2,1)S(1)} %dynamic-update-slice.1), channel_id=1, replica_groups=mesh['dp'=16,'tensor'=2] {'dp'}, use_global_device_ids=true, to_apply=%add | all-reduce | flops 1536 | bytes 6144
  57.4 41.6 %all_gather.39 = bf16[384,768]{0,1:T(8,128)(2,1)} all-gather(bf16[384,48]{0,1:T(8,128)(2,1)S(1)} %copy-done.31), channel_id=1, replica_groups=mesh['dp'=16,'tensor'=2] {'dp'}, dimensions={1}, use_global_device_ids=true | all-gather | bytes 626688 | tf_op jit(solution)/shard_map/all_gather | solution.py:65
  99.1 25.5 %all-gather.9.cloned.1.call-done = bf16[768,3,384]{2,0,1:T(8,128)(2,1)} async-done(((bf16[48,3,384]{2,0,1:T(8,128)(2,1)}), bf16[768,3,384]{2,0,1:T(8,128)(2,1)}) %all-gather.9.cloned.1.call-update) | async-done | bytes 1769488 | tf_op jit(solution)/shard_map/all_gather | solution.py:64
  124.5 4.0 fusion.68
  132.2 25.0 %while.27 = (s32[]{:T(128)}, bf16[2,512,6,64]{1,3,2,0:T(8,128)(2,1)S(1)}, f32[2,6,512]{2,1,0:T(8,128)S(1)}, s32[2,512]{1,0:T(2,128)S(1)}, s32[1024]{0:T(1024)S(1...) while((s32[]{:T(128)}, ...), condition=%wide.region_6.7_spmd, body=%wide.region_3.6_spmd.sunk | while | flops 843576320 | bytes 42727540 | solution.py:157
  132.6 3.4 fusion.129
  136.0 3.6 fusion.130
  139.6 5.1 fusion.131
  145.1 3.4 fusion.129
  148.5 3.6 fusion.130
  152.2 5.1 fusion.131
  159.1 2.2 convolution_convert_fusion.1
  161.4 2.4 convert_element_type.94
  164.6 4.7 reduce-scatter.9.cloned.1.call-done
  173.0 51.0 %all_gather.43 = bf16[576,768]{0,1:T(8,128)(2,1)} all-gather(bf16[576,48]{0,1:T(8,128)(2,1)S(1)} %copy-done.30), channel_id=1, replica_groups=mesh['dp'=16,'tensor'=2] {'dp'}, dimensions={1}, use_global_device_ids=true | all-gather | bytes 940032 | tf_op jit(solution)/shard_map/all_gather | solution.py:81
  224.1 2.8 fusion.85
  226.9 20.7 %all-gather.13.cloned.1.call-done = bf16[768,2,576]{2,0,1:T(8,128)(2,1)} async-done(((bf16[48,2,576]{2,0,1:T(8,128)(2,1)}), bf16[768,2,576]{2,0,1:T(8,128)(2,1)}) %all-gather.13.cloned.1.call-update) | async-done | bytes 1769488 | tf_op jit(solution)/shard_map/all_gather | solution.py:80
  247.6 10.5 %all-gather.11.cloned.1.call-done = bf16[1024,768]{1,0:T(8,128)(2,1)} async-done(((bf16[512,768]{1,0:T(8,128)(2,1)}), bf16[1024,768]{1,0:T(8,128)(2,1)}) %all-gather.11.cloned.1.call-update) | async-done | bytes 1572880 | tf_op jit(solution)/shard_map/all_gather | solution.py:95
  258.1 4.1 fusion.64
  262.3 5.6 fusion.71
  267.9 2.3 fusion.70
  271.3 3.5 bitcast_convert_fusion.1
  274.9 2.7 convolution_convert_fusion
  277.6 7.6 reduce-scatter.13.cloned.1.call-done
  285.2 2.5 fusion.60
  287.7 10.0 %reduce-scatter.11.cloned.1.call-done = bf16[512,768]{1,0:T(8,128)(2,1)} async-done(((bf16[1024,768]{1,0:T(8,128)(2,1)}), bf16[512,768]{1,0:T(8,128)(2,1)}) %reduce-scatter.11.cloned.1.call-update) | async-done | bytes 786448 | tf_op jit(solution)/shard_map/reduce_scatter | solution.py:107
  297.7 3.1 fusion.81
  303.6 5.8 fusion.62
  309.5 4.8 all-gather.17.cloned.1.call-done
  314.3 3.3 convolution_convert_fusion.2
  320.5 2.2 copy.58
  322.7 89.6 %while.28 = (s32[]{:T(128)}, f32[1024,6,64]{0,2,1:T(8,128)S(1)}, f32[1024,6,64]{0,2,1:T(8,128)}, f32[2,512,6,64]{1,0,3,2:T(2,128)}, bf16[2,512,6,64]{1,3,2,0:T(8...) while((s32[]{:T(128)}, f32[1024,6,64]{0,2,1:T(8,128)S(1)}, ...), condition=%wide.region_16.17_spmd.clone, body=%wide.region_14.16_spmd.clone.sunk | while | flops 2063135744 | bytes 110721200 | solution.py:208
  323.3 2.8 fusion.141
  326.1 5.5 bitcast_add_fusion.5
  331.6 8.4 multiply_reduce_fusion.4
  340.0 7.0 multiply_convert_fusion.6
  347.0 2.0 fusion.142
  349.0 2.4 bitcast_add_fusion.4
  352.2 15.0 %dynamic_update_slice.19 = f32[2,512,6,64]{1,0,3,2:T(2,128)} dynamic-update-slice(f32[2,512,6,64]{1,0,3,2:T(2,128)} %get-tuple-element.475, f32[1,512,6,64]{1,0,3,2:T(1,128)S(1)} %copy.88, s32[]{:T(128)S(6)} %copy.108, s32[]{:T(128)} %constant.64.clone.1..sunk, s32[]{:T(128)} %constant.64.clone.1..sunk, s32[]{:T(128)} %constant.64.clone.1..sunk) | dynamic-update-slice | bytes 1572868 | tf_op jit(solution)/shard_map/while/body/jit(dynamic_update_index_in_dim)/dynamic_update_slice | solution.py:157
  367.6 2.8 fusion.141
  370.5 6.1 bitcast_add_fusion.5
  376.5 8.5 multiply_reduce_fusion.4
  385.0 6.9 multiply_convert_fusion.6
  391.9 2.0 fusion.142
  393.9 2.4 bitcast_add_fusion.4
  397.1 15.0 %dynamic_update_slice.19 = f32[2,512,6,64]{1,0,3,2:T(2,128)} dynamic-update-slice(f32[2,512,6,64]{1,0,3,2:T(2,128)} %get-tuple-element.475, f32[1,512,6,64]{1,0,3,2:T(1,128)S(1)} %copy.88, s32[]{:T(128)S(6)} %copy.108, s32[]{:T(128)} %constant.64.clone.1..sunk, s32[]{:T(128)} %constant.64.clone.1..sunk, s32[]{:T(128)} %constant.64.clone.1..sunk) | dynamic-update-slice | bytes 1572868 | tf_op jit(solution)/shard_map/while/body/jit(dynamic_update_index_in_dim)/dynamic_update_slice | solution.py:157
  412.4 3.5 reshape.252
  415.9 1.8 add_convert_fusion.1
  418.6 1.5 convert.56
  421.3 5.2 bitcast_convert_fusion
  426.6 4.3 fusion.87
  431.0 3.6 fusion.86
  434.6 5.4 fusion.66
  440.8 16.0 %reduce-scatter.21.cloned.1.call-done = f32[48,2,576]{2,0,1:T(8,128)} async-done(((f32[768,2,576]{2,0,1:T(8,128)}), f32[48,2,576]{2,0,1:T(8,128)}) %reduce-scatter.21.cloned.1.call-update) | async-done | bytes 221200 | tf_op jit(solution)/shard_map/reduce_scatter | solution.py:267
  456.8 1.8 copy.65
  458.6 9.5 %reduce-scatter.15.cloned.1.call-done = bf16[512,768]{1,0:T(8,128)(2,1)} async-done(((bf16[1024,768]{1,0:T(8,128)(2,1)}), bf16[512,768]{1,0:T(8,128)(2,1)}) %reduce-scatter.15.cloned.1.call-update) | async-done | bytes 786448 | tf_op jit(solution)/shard_map/reduce_scatter | solution.py:120
  468.1 1.6 fusion.58
  470.6 42.8 %all-reduce.4 = (f32[768]{0:T(1024)S(1)}, f32[768]{0:T(1024)S(1)}) all-reduce(f32[768]{0:T(1024)S(1)} %get-tuple-element.227, f32[768]{0:T(1024)S(1)} %copy-done.38), channel_id=10, replica_groups=mesh['dp'=16,'tensor'=2] {'dp'}, use_global_device_ids=true, to_apply=%region_25.26.clone | all-reduce | flops 1536 | bytes 12288
  513.5 3.0 all-reduce.5
  516.5 3.7 add_add_fusion.2
  520.2 80.6 %reduce-scatter.23.cloned.1.call-done = f32[576,48]{0,1:T(8,128)} async-done(((f32[576,768]{0,1:T(8,128)}), f32[576,48]{0,1:T(8,128)}) %reduce-scatter.23.cloned.1.call-update) | async-done | bytes 110608 | tf_op jit(solution)/shard_map/reduce_scatter | solution.py:268
  600.8 128.6 %reduce-scatter.19.cloned.1.call-done = f32[384,48]{0,1:T(8,128)} async-done(((f32[384,768]{0,1:T(8,128)}), f32[384,48]{0,1:T(8,128)}) %reduce-scatter.19.cloned.1.call-update) | async-done | bytes 73744 | tf_op jit(solution)/shard_map/reduce_scatter | solution.py:307
  729.4 138.9 %reduce-scatter.17.cloned.1.call-done = f32[48,3,384]{2,0,1:T(8,128)} async-done(((f32[768,3,384]{2,0,1:T(8,128)}), f32[48,3,384]{2,0,1:T(8,128)}) %reduce-scatter.17.cloned.1.call-update) | async-done | bytes 221200 | tf_op jit(solution)/shard_map/reduce_scatter | solution.py:306
  (181 shorter events, 27.5 us)
Async XLA Ops:
  7.2 2.2 copy-start.39
  7.2 1.9 copy-start
  7.2 3.5 copy-start.42
  7.2 3.7 copy-start.43
  7.2 91.8 %all-gather.7.cloned.1.call-start = ((), (), s32[]{:S(2)}) async-start(), calls=%async_computation.8 | async-start | bytes 2359296 | tf_op jit(solution)/shard_map/all_gather | solution.py:95
  9.1 46.8 %copy-start.28 = (f32[512]{0:T(512)}, f32[512]{0:T(512)S(1)}, u32[]{:S(2)}) copy-start(f32[512]{0:T(512)S(1)} %broadcast_multiply_fusion.1) | copy-start | bytes 6148
  9.1 47.6 %copy-start.40 = (s32[1,16]{1,0:T(1,128)S(1)}, s32[1,16]{1,0:T(1,128)}, u32[]{:S(2)}) copy-start(s32[1,16]{1,0:T(1,128)} %param.14) | copy-start | bytes 196
  9.1 48.3 %copy-start.31 = (bf16[384,48]{0,1:T(8,128)(2,1)S(1)}, bf16[384,48]{0,1:T(8,128)(2,1)}, u32[]{:S(2)}) copy-start(bf16[384,48]{0,1:T(8,128)(2,1)} %param.16) | copy-start | bytes 110596
  9.4 45.3 %copy-start.36 = (f32[512]{0:T(512)}, f32[512]{0:T(512)S(1)}, u32[]{:S(2)}) copy-start(f32[512]{0:T(512)S(1)} %multiply_reduce_fusion.2) | copy-start | bytes 6148
  9.4 47.4 %copy-start.32 = (f32[512]{0:T(512)}, f32[512]{0:T(512)S(1)}, u32[]{:S(2)}) copy-start(f32[512]{0:T(512)S(1)} %fusion.74) | copy-start | bytes 6148
  54.7 2.1 copy-start.26
  55.9 68.7 %all-gather.9.cloned.1.call-start = ((), (), s32[]{:S(2)}) async-start(), calls=%async_computation.9 | async-start | bytes 1880064 | tf_op jit(solution)/shard_map/all_gather | solution.py:64
  56.6 112.7 %reduce-scatter.9.cloned.1.call-start = ((), (), s32[]{:S(2)}) async-start(), calls=%async_computation.10 | async-start | bytes 2359296 | tf_op jit(solution)/shard_map/reduce_scatter | solution.py:107
  57.4 72.6 %copy-start.12 = (f32[1024,32]{0,1:T(8,128)}, f32[1024,32]{0,1:T(8,128)S(1)}, u32[]{:S(2)}) copy-start(f32[1024,32]{0,1:T(8,128)S(1)} %get-tuple-element.302) | copy-start | bytes 393220
  57.4 72.6 %copy-start.14 = (f32[1024,32]{0,1:T(8,128)}, f32[1024,32]{0,1:T(8,128)S(1)}, u32[]{:S(2)}) copy-start(f32[1024,32]{0,1:T(8,128)S(1)} %get-tuple-element.303) | copy-start | bytes 393220
  157.2 4.0 copy-start.23
  157.3 1.9 copy-start.21
  158.2 0.9 copy-start.18
  161.3 2.5 copy-start.25
  161.3 62.8 %all-gather.15.cloned.1.call-start = ((), (), s32[]{:S(2)}) async-start(), calls=%async_computation.14 | async-start | bytes 2359296 | tf_op jit(solution)/shard_map/all_gather | solution.py:99
  163.8 83.8 %all-gather.13.cloned.1.call-start = ((), (), s32[]{:S(2)}) async-start(), calls=%async_computation.12 | async-start | bytes 2088960 | tf_op jit(solution)/shard_map/all_gather | solution.py:80
  164.5 93.6 %all-gather.11.cloned.1.call-start = ((), (), s32[]{:S(2)}) async-start(), calls=%async_computation.11 | async-start | bytes 2359296 | tf_op jit(solution)/shard_map/all_gather | solution.py:95
  170.7 1.1 copy-start.2
  170.7 2.4 copy-start.30
  173.0 112.2 %reduce-scatter.13.cloned.1.call-start = ((), (), s32[]{:S(2)}) async-start(), calls=%async_computation.15 | async-start | bytes 2359296 | tf_op jit(solution)/shard_map/reduce_scatter | solution.py:120
  267.9 2.3 copy-start.16
  267.9 3.3 copy-start.41
  270.2 1.0 copy-start.10
  271.3 3.6 copy-start.8
  271.3 3.6 copy-start.17
  274.8 22.9 %reduce-scatter.11.cloned.1.call-start = ((), (), s32[]{:S(2)}) async-start(), calls=%async_computation.13 | async-start | bytes 2359296 | tf_op jit(solution)/shard_map/reduce_scatter | solution.py:107
  277.5 7.7 copy-start.3
  277.6 36.7 %all-gather.17.cloned.1.call-start = ((), (), s32[]{:S(2)}) async-start(), calls=%async_computation.16 | async-start | bytes 2359296 | tf_op jit(solution)/shard_map/all_gather | solution.py:99
  285.2 12.5 %copy-start.7 = (bf16[512,768]{1,0:T(8,128)(2,1)S(1)}, bf16[512,768]{1,0:T(8,128)(2,1)}, u32[]{:S(2)}) copy-start(bf16[512,768]{1,0:T(8,128)(2,1)} %reduce-scatter.13.cloned.1.call-done) | copy-start | bytes 2359300
  297.7 4.3 copy-start.4
  300.8 1.2 copy-start.5
  300.8 1.2 copy-start.34
  302.0 1.6 copy-start.11
  303.1 153.7 %reduce-scatter.21.cloned.1.call-start = ((), (), s32[]{:S(2)}) async-start(), calls=%async_computation.20 | async-start | bytes 4177920 | tf_op jit(solution)/shard_map/reduce_scatter | solution.py:267
  309.4 4.9 copy-start.22
  309.4 158.6 %reduce-scatter.15.cloned.1.call-start = ((), (), s32[]{:S(2)}) async-start(), calls=%async_computation.17 | async-start | bytes 2359296 | tf_op jit(solution)/shard_map/reduce_scatter | solution.py:120
  317.6 5.1 copy-start.24
  412.3 3.5 copy-start.13
  412.3 3.5 copy-start.15
  421.3 5.3 copy-start.9
  426.5 4.4 copy-start.19
  426.6 174.3 %reduce-scatter.23.cloned.1.call-start = ((), (), s32[]{:S(2)}) async-start(), calls=%async_computation.21 | async-start | bytes 2088960 | tf_op jit(solution)/shard_map/reduce_scatter | solution.py:268
  430.9 3.7 copy-start.20
  430.9 298.5 %reduce-scatter.19.cloned.1.call-start = ((), (), s32[]{:S(2)}) async-start(), calls=%async_computation.19 | async-start | bytes 1253376 | tf_op jit(solution)/shard_map/reduce_scatter | solution.py:307
  434.6 433.8 %reduce-scatter.17.cloned.1.call-start = ((), (), s32[]{:S(2)}) async-start(), calls=%async_computation.18 | async-start | bytes 3760128 | tf_op jit(solution)/shard_map/reduce_scatter | solution.py:306
  440.0 28.0 %copy-start.1 = (f32[512,768]{1,0:T(8,128)S(1)}, f32[512,768]{1,0:T(8,128)}, u32[]{:S(2)}) copy-start(f32[512,768]{1,0:T(8,128)} %param.13) | copy-start | bytes 4718596
  440.0 28.0 %copy-start.27 = (f32[768]{0:T(1024)S(1)}, f32[768]{0:T(1024)}, u32[]{:S(2)}) copy-start(f32[768]{0:T(1024)} %copy-done.26) | copy-start | bytes 9220
  440.0 28.0 %copy-start.29 = (f32[512]{0:T(512)S(1)}, f32[512]{0:T(512)}, u32[]{:S(2)}) copy-start(f32[512]{0:T(512)} %copy-done.28) | copy-start | bytes 6148
  440.0 29.6 %copy-start.37 = (f32[512]{0:T(512)S(1)}, f32[512]{0:T(512)}, u32[]{:S(2)}) copy-start(f32[512]{0:T(512)} %copy-done.36) | copy-start | bytes 6148
  440.1 29.6 %copy-start.33 = (f32[512]{0:T(512)S(1)}, f32[512]{0:T(512)}, u32[]{:S(2)}) copy-start(f32[512]{0:T(512)} %copy-done.32) | copy-start | bytes 6148
  458.6 12.0 %copy-start.38 = (f32[768]{0:T(1024)S(1)}, f32[768]{0:T(1024)}, u32[]{:S(2)}) copy-start(f32[768]{0:T(1024)} %get-tuple-element.229) | copy-start | bytes 9220
  458.6 57.9 %copy-start.35 = (f32[512]{0:T(512)S(1)}, f32[512]{0:T(512)}, u32[]{:S(2)}) copy-start(f32[512]{0:T(512)} %copy-done.34) | copy-start | bytes 6148
  468.1 1.6 copy-start.6
Sparse Core Ops, SparseCore 0:
  56.0 5.6 all-gather.6
  64.4 60.1 all-gather.8
  161.4 7.8 reduce-scatter.8
  170.8 10.9 all-gather.14
  185.3 62.2 all-gather.12
  249.7 8.4 all-gather.10
  274.9 10.2 reduce-scatter.12
  287.4 10.2 reduce-scatter.10
  303.3 10.9 all-gather.16
  320.1 136.6 reduce-scatter.20
  459.7 8.2 reduce-scatter.14
  473.3 127.4 reduce-scatter.22
  606.9 122.5 reduce-scatter.18
  735.8 132.5 reduce-scatter.16
where the time goes:
time: 888 us; the launch traced here: 875 us
  waiting for transfers between devices  458 us (52%)
  blocking collectives  182 us (20%)
  matrix products  107 us (12%)
  other arithmetic  56.4 us (6%)
  local copies, waits for them, and re-layouts  54.4 us (6%)
  between operations  16.3 us (2%)
    reduce_scatter x1, waiting for transfers between devices, shards(): lax.psum_scatter(grad_qkv, 'dp', scatter_dimension=0, tiled=True)  139 us
    reduce_scatter x1, waiting for transfers between devices, shards(): lax.psum_scatter(grad_attn_out, 'dp', scatter_dimension=1, tiled=True)  129 us
    unnamed x2, blocking collectives  86.3 us
    reduce_scatter x1, waiting for transfers between devices, shards(): lax.psum_scatter(grad_mlp_out, 'dp', scatter_dimension=1, tiled=True)  80.6 us
    all_gather x1, blocking collectives, fetch_mlp(): lax.all_gather(w_mlp_out, 'dp', axis=1, tiled=True)  51 us
    all_gather x1, blocking collectives, fetch_attention(): lax.all_gather(w_attn_out, 'dp', axis=1, tiled=True)  41.6 us
    dynamic_update_slice x4, local copies, waits for them, and re-layouts, attention_forward(): lax.map(one_block, (queries.reshape(block_count, block_rows, heads_here,...  31.7 us
    all_gather x1, waiting for transfers between devices, fetch_attention(): lax.all_gather(w_qkv, 'dp', axis=0, tiled=True)  25.5 us
  transfers between devices with their start and end apart: 14, of which 12 were waited for; matrix products, arithmetic and copies ran while one was open for 18% of the time, Pallas kernels for 0%

commit v1 on v0

--- a/solution.py
+++ b/solution.py
@@ -78,7 +78,9 @@
 def fetch_mlp(w_in, w_mlp_out, gain_mlp):
     return (
         lax.all_gather(w_in, "dp", axis=0, tiled=True),
-        lax.all_gather(w_mlp_out, "dp", axis=1, tiled=True),
+        jnp.concatenate(
+            lax.all_to_all(jnp.stack(lax.axis_size("dp") * [w_mlp_out]), "dp", 0, 0), axis=1
+        ),
         lax.all_gather(gain_mlp, "dp", axis=0, tiled=True),
     )
 

time: 888 us -> 894 us (level)
  waiting for transfers between devices: 458 us -> 433 us
  blocking collectives: 182 us -> 194 us
    all_gather x1, waiting for transfers between devices: 20.7 us -> 5.8 us  [fetch_mlp(): lax.all_gather(w_in, 'dp', axis=0, tiled=True)]
    all_gather x1, blocking collectives: 51 us -> 63.1 us  [fetch_mlp_again(): lax.all_gather(w_mlp_out, 'dp', axis=1, tiled=True)]
  transfers between devices with their start and end apart: 14 -> 15, of which waited for: 12 -> 12; matrix products, arithmetic and copies ran while one was open for 18% -> 20% of each run, Pallas kernels for 0% -> 0%
where the time goes in v1:
time: 894 us; the launch traced here: 881 us
  waiting for transfers between devices  433 us (48%)
  blocking collectives  194 us (22%)
  matrix products  115 us (13%)
  local copies, waits for them, and re-layouts  58.4 us (7%)
  other arithmetic  55 us (6%)
  between operations  16.4 us (2%)
    reduce_scatter x1, waiting for transfers between devices, shards(): lax.psum_scatter(grad_qkv, 'dp', scatter_dimension=0, tiled=True)  139 us
    reduce_scatter x1, waiting for transfers between devices, shards(): lax.psum_scatter(grad_attn_out, 'dp', scatter_dimension=1, tiled=True)  129 us
    unnamed x2, blocking collectives  86.3 us
    reduce_scatter x1, waiting for transfers between devices, shards(): lax.psum_scatter(grad_mlp_out, 'dp', scatter_dimension=1, tiled=True)  80.4 us
    all_gather x1, blocking collectives, fetch_mlp_again(): lax.all_gather(w_mlp_out, 'dp', axis=1, tiled=True)  63.1 us
    all_gather x1, blocking collectives, fetch_attention(): lax.all_gather(w_attn_out, 'dp', axis=1, tiled=True)  41.6 us
    dynamic_update_slice x4, local copies, waits for them, and re-layouts, attention_forward(): lax.map(one_block, (queries.reshape(block_count, block_rows, heads_here,...  31.5 us
    all_gather x1, waiting for transfers between devices, fetch_attention(): lax.all_gather(w_qkv, 'dp', axis=0, tiled=True)  25.5 us
  transfers between devices with their start and end apart: 15, of which 12 were waited for; matrix products, arithmetic and copies ran while one was open for 20% of the time, Pallas kernels for 0%

profile of v1, /device:TPU:0, one launch (start us, length us, event | category | flops | bytes accessed | tf_op | source)
XLA Modules:
  0.0 880.7 jit_solution(18129527226678899810)
XLA Ops:
  7.3 1.7 reduce_sum.107
  11.2 43.5 %all-reduce.6 = (bf16[768]{0:T(1024)(128)(2,1)S(1)}, bf16[768]{0:T(1024)(128)(2,1)S(1)}) all-reduce(bf16[768]{0:T(1024)(128)(2,1)S(1)} %dynamic-update-slice, bf16[768]{0:T(1024)(128)(2,1)S(1)} %dynamic-update-slice.1), channel_id=1, replica_groups=mesh['dp'=16,'tensor'=2] {'dp'}, use_global_device_ids=true, to_apply=%add | all-reduce | flops 1536 | bytes 6144
  57.4 41.6 %all_gather.38 = bf16[384,768]{0,1:T(8,128)(2,1)} all-gather(bf16[384,48]{0,1:T(8,128)(2,1)S(1)} %copy-done.33), channel_id=1, replica_groups=mesh['dp'=16,'tensor'=2] {'dp'}, dimensions={1}, use_global_device_ids=true | all-gather | bytes 626688 | tf_op jit(solution)/shard_map/all_gather | solution.py:65
  99.1 25.5 %all-gather.9.cloned.1.call-done = bf16[768,3,384]{2,0,1:T(8,128)(2,1)} async-done(((bf16[48,3,384]{2,0,1:T(8,128)(2,1)}), bf16[768,3,384]{2,0,1:T(8,128)(2,1)}) %all-gather.9.cloned.1.call-update) | async-done | bytes 1769488 | tf_op jit(solution)/shard_map/all_gather | solution.py:64
  124.5 4.0 fusion.79
  132.2 25.0 %while.27 = (s32[]{:T(128)}, bf16[2,512,6,64]{1,3,2,0:T(8,128)(2,1)S(1)}, f32[2,6,512]{2,1,0:T(8,128)S(1)}, s32[2,512]{1,0:T(2,128)S(1)}, s32[1024]{0:T(1024)S(1...) while((s32[]{:T(128)}, ...), condition=%wide.region_6.7_spmd, body=%wide.region_3.6_spmd.sunk | while | flops 843576320 | bytes 42727540 | solution.py:159
  132.6 3.4 fusion.172
  135.9 3.6 fusion.173
  139.6 5.1 fusion.174
  145.1 3.4 fusion.172
  148.4 3.6 fusion.173
  152.1 5.1 fusion.174
  159.0 2.2 convolution_convert_fusion.1
  161.3 2.4 convert_element_type.100
  164.5 4.7 reduce-scatter.9.cloned.1.call-done
  173.9 7.2 all-to-all-start
  181.2 63.1 %all_gather.43 = bf16[576,768]{0,1:T(8,128)(2,1)} all-gather(bf16[576,48]{0,1:T(8,128)(2,1)S(1)} %copy-done.25), channel_id=1, replica_groups=mesh['dp'=16,'tensor'=2] {'dp'}, dimensions={1}, use_global_device_ids=true | all-gather | bytes 940032 | tf_op jit(solution)/shard_map/all_gather | solution.py:91
  244.3 2.8 fusion.131
  247.2 5.8 all-gather.13.cloned.1.call-done
  252.9 11.3 %all-gather.11.cloned.1.call-done = bf16[1024,768]{1,0:T(8,128)(2,1)} async-done(((bf16[512,768]{1,0:T(8,128)(2,1)}), bf16[1024,768]{1,0:T(8,128)(2,1)}) %all-gather.11.cloned.1.call-update) | async-done | bytes 1572880 | tf_op jit(solution)/shard_map/all_gather | solution.py:97
  264.2 4.1 fusion.75
  268.3 5.6 fusion.86
  277.0 3.5 bitcast_convert_fusion.1
  280.5 9.4 %convolution_convert_fusion = bf16[1024,768]{1,0:T(8,128)(2,1)} fusion(bf16[576,768]{0,1:T(8,128)(2,1)} %bitcast.15, f32[1024,2,576]{0,2,1:T(8,128)} %copy-done.6), kind=kOutput, calls=%fused_computation.111 | convolution fusion | flops 945684480 | bytes 7176192 | tf_op jit(solution)/shard_map/dot_general | solution.py:107
  291.4 2.5 fusion.71
  294.0 9.4 %reduce-scatter.11.cloned.1.call-done = bf16[512,768]{1,0:T(8,128)(2,1)} async-done(((bf16[1024,768]{1,0:T(8,128)(2,1)}), bf16[512,768]{1,0:T(8,128)(2,1)}) %reduce-scatter.11.cloned.1.call-update) | async-done | bytes 786448 | tf_op jit(solution)/shard_map/reduce_scatter | solution.py:109
  303.4 3.1 fusion.127
  309.3 5.9 fusion.73
  315.2 4.8 all-gather.17.cloned.1.call-done
  320.0 3.3 convolution_convert_fusion.2
  324.7 1.5 reshape_reshape.4
  326.1 2.1 copy.59
  328.3 89.5 %while.28 = (s32[]{:T(128)}, f32[1024,6,64]{0,2,1:T(8,128)S(1)}, f32[1024,6,64]{0,2,1:T(8,128)}, f32[2,512,6,64]{1,0,3,2:T(2,128)}, bf16[2,512,6,64]{1,3,2,0:T(8...) while((s32[]{:T(128)}, f32[1024,6,64]{0,2,1:T(8,128)S(1)}, ...), condition=%wide.region_16.17_spmd.clone, body=%wide.region_14.16_spmd.clone.sunk | while | flops 2063135744 | bytes 110721200 | solution.py:210
  328.8 2.8 fusion.184
  331.7 5.5 bitcast_add_fusion.5
  337.2 8.5 multiply_reduce_fusion.4
  345.6 7.0 multiply_convert_fusion.5
  352.6 2.0 fusion.185
  354.6 2.4 bitcast_add_fusion.4
  357.8 14.9 %dynamic_update_slice.19 = f32[2,512,6,64]{1,0,3,2:T(2,128)} dynamic-update-slice(f32[2,512,6,64]{1,0,3,2:T(2,128)} %get-tuple-element.473, f32[1,512,6,64]{1,0,3,2:T(1,128)S(1)} %copy.89, s32[]{:T(128)S(6)} %copy.109, s32[]{:T(128)} %constant.64.clone.1..sunk, s32[]{:T(128)} %constant.64.clone.1..sunk, s32[]{:T(128)} %constant.64.clone.1..sunk) | dynamic-update-slice | bytes 1572868 | tf_op jit(solution)/shard_map/while/body/jit(dynamic_update_index_in_dim)/dynamic_update_slice | solution.py:159
  373.1 2.8 fusion.184
  376.0 6.1 bitcast_add_fusion.5
  382.0 8.5 multiply_reduce_fusion.4
  390.5 6.9 multiply_convert_fusion.5
  397.4 2.0 fusion.185
  399.5 2.4 bitcast_add_fusion.4
  402.7 14.9 %dynamic_update_slice.19 = f32[2,512,6,64]{1,0,3,2:T(2,128)} dynamic-update-slice(f32[2,512,6,64]{1,0,3,2:T(2,128)} %get-tuple-element.473, f32[1,512,6,64]{1,0,3,2:T(1,128)S(1)} %copy.89, s32[]{:T(128)S(6)} %copy.109, s32[]{:T(128)} %constant.64.clone.1..sunk, s32[]{:T(128)} %constant.64.clone.1..sunk, s32[]{:T(128)} %constant.64.clone.1..sunk) | dynamic-update-slice | bytes 1572868 | tf_op jit(solution)/shard_map/while/body/jit(dynamic_update_index_in_dim)/dynamic_update_slice | solution.py:159
  417.8 3.5 reshape.263
  421.3 1.8 add_convert_fusion.1
  425.7 1.6 convert.56
  428.4 5.7 bitcast_convert_fusion
  434.2 5.7 fusion.82
  440.1 3.6 fusion.132
  443.8 5.4 fusion.77
  450.0 12.5 %reduce-scatter.21.cloned.1.call-done = f32[48,2,576]{2,0,1:T(8,128)} async-done(((f32[768,2,576]{2,0,1:T(8,128)}), f32[48,2,576]{2,0,1:T(8,128)}) %reduce-scatter.21.cloned.1.call-update) | async-done | bytes 221200 | tf_op jit(solution)/shard_map/reduce_scatter | solution.py:269
  462.5 1.8 copy.66
  464.2 9.5 %reduce-scatter.15.cloned.1.call-done = bf16[512,768]{1,0:T(8,128)(2,1)} async-done(((bf16[1024,768]{1,0:T(8,128)(2,1)}), bf16[512,768]{1,0:T(8,128)(2,1)}) %reduce-scatter.15.cloned.1.call-update) | async-done | bytes 786448 | tf_op jit(solution)/shard_map/reduce_scatter | solution.py:122
  473.7 1.6 fusion.69
  476.3 42.8 %all-reduce.4 = (f32[768]{0:T(1024)S(1)}, f32[768]{0:T(1024)S(1)}) all-reduce(f32[768]{0:T(1024)S(1)} %get-tuple-element.227, f32[768]{0:T(1024)S(1)} %copy-done.40), channel_id=10, replica_groups=mesh['dp'=16,'tensor'=2] {'dp'}, use_global_device_ids=true, to_apply=%region_25.26.clone | all-reduce | flops 1536 | bytes 12288
  519.2 3.0 all-reduce.5
  522.1 3.7 add_add_fusion.2
  525.8 80.4 %reduce-scatter.23.cloned.1.call-done = f32[576,48]{0,1:T(8,128)} async-done(((f32[576,768]{0,1:T(8,128)}), f32[576,48]{0,1:T(8,128)}) %reduce-scatter.23.cloned.1.call-update) | async-done | bytes 110608 | tf_op jit(solution)/shard_map/reduce_scatter | solution.py:270
  606.3 128.6 %reduce-scatter.19.cloned.1.call-done = f32[384,48]{0,1:T(8,128)} async-done(((f32[384,768]{0,1:T(8,128)}), f32[384,48]{0,1:T(8,128)}) %reduce-scatter.19.cloned.1.call-update) | async-done | bytes 73744 | tf_op jit(solution)/shard_map/reduce_scatter | solution.py:309
  734.9 138.9 %reduce-scatter.17.cloned.1.call-done = f32[48,3,384]{2,0,1:T(8,128)} async-done(((f32[768,3,384]{2,0,1:T(8,128)}), f32[48,3,384]{2,0,1:T(8,128)}) %reduce-scatter.17.cloned.1.call-update) | async-done | bytes 221200 | tf_op jit(solution)/shard_map/reduce_scatter | solution.py:308
  (188 shorter events, 32.0 us)
Async XLA Ops:
  7.2 2.2 copy-start.41
  7.2 1.9 copy-start
  7.2 3.5 copy-start.44
  7.2 3.7 copy-start.45
  7.2 91.8 %all-gather.7.cloned.1.call-start = ((), (), s32[]{:S(2)}) async-start(), calls=%async_computation.9 | async-start | bytes 2359296 | tf_op jit(solution)/shard_map/all_gather | solution.py:97
  9.1 46.8 %copy-start.31 = (f32[512]{0:T(512)}, f32[512]{0:T(512)S(1)}, u32[]{:S(2)}) copy-start(f32[512]{0:T(512)S(1)} %broadcast_multiply_fusion.1) | copy-start | bytes 6148
  9.1 47.6 %copy-start.42 = (s32[1,16]{1,0:T(1,128)S(1)}, s32[1,16]{1,0:T(1,128)}, u32[]{:S(2)}) copy-start(s32[1,16]{1,0:T(1,128)} %param.14) | copy-start | bytes 196
  9.1 48.3 %copy-start.33 = (bf16[384,48]{0,1:T(8,128)(2,1)S(1)}, bf16[384,48]{0,1:T(8,128)(2,1)}, u32[]{:S(2)}) copy-start(bf16[384,48]{0,1:T(8,128)(2,1)} %param.16) | copy-start | bytes 110596
  9.4 45.3 %copy-start.38 = (f32[512]{0:T(512)}, f32[512]{0:T(512)S(1)}, u32[]{:S(2)}) copy-start(f32[512]{0:T(512)S(1)} %multiply_reduce_fusion.2) | copy-start | bytes 6148
  9.4 47.4 %copy-start.34 = (f32[512]{0:T(512)}, f32[512]{0:T(512)S(1)}, u32[]{:S(2)}) copy-start(f32[512]{0:T(512)S(1)} %fusion.89) | copy-start | bytes 6148
  54.7 2.1 copy-start.29
  55.9 68.7 %all-gather.9.cloned.1.call-start = ((), (), s32[]{:S(2)}) async-start(), calls=%async_computation.10 | async-start | bytes 1880064 | tf_op jit(solution)/shard_map/all_gather | solution.py:64
  56.6 112.6 %reduce-scatter.9.cloned.1.call-start = ((), (), s32[]{:S(2)}) async-start(), calls=%async_computation.11 | async-start | bytes 2359296 | tf_op jit(solution)/shard_map/reduce_scatter | solution.py:109
  57.4 72.6 %copy-start.11 = (f32[1024,32]{0,1:T(8,128)}, f32[1024,32]{0,1:T(8,128)S(1)}, u32[]{:S(2)}) copy-start(f32[1024,32]{0,1:T(8,128)S(1)} %get-tuple-element.300) | copy-start | bytes 393220
  57.4 72.6 %copy-start.13 = (f32[1024,32]{0,1:T(8,128)}, f32[1024,32]{0,1:T(8,128)S(1)}, u32[]{:S(2)}) copy-start(f32[1024,32]{0,1:T(8,128)S(1)} %get-tuple-element.301) | copy-start | bytes 393220
  157.2 4.0 copy-start.26
  157.2 1.8 copy-start.23
  158.1 0.9 copy-start.18
  161.2 2.5 copy-start.28
  161.2 83.1 %all-gather.15.cloned.1.call-start = ((), (), s32[]{:S(2)}) async-start(), calls=%async_computation.15 | async-start | bytes 2359296 | tf_op jit(solution)/shard_map/all_gather | solution.py:101
  163.7 89.3 %all-gather.13.cloned.1.call-start = ((), (), s32[]{:S(2)}) async-start(), calls=%async_computation.13 | async-start | bytes 2088960 | tf_op jit(solution)/shard_map/all_gather | solution.py:80
  164.4 99.8 %all-gather.11.cloned.1.call-start = ((), (), s32[]{:S(2)}) async-start(), calls=%async_computation.12 | async-start | bytes 2359296 | tf_op jit(solution)/shard_map/all_gather | solution.py:97
  170.6 1.1 copy-start.2
  170.6 2.3 copy-start.25
  173.9 106.6 %all-to-all-start = ((bf16[16,576,48]{1,2,0:T(8,128)(2,1)}), bf16[16,576,48]{1,2,0:T(8,128)(2,1)}, u32[]{:S(2)}, u32[]{:S(2)}) async-start(bf16[16,576,48]{1,2,0:T(8,128)(2,1)} %stack.19), calls=%async_computation.1 | async-start | bytes 1966080 | tf_op jit(solution)/shard_map/all_to_all | solution.py:82
  181.1 109.7 %reduce-scatter.13.cloned.1.call-start = ((), (), s32[]{:S(2)}) async-start(), calls=%async_computation.16 | async-start | bytes 2359296 | tf_op jit(solution)/shard_map/reduce_scatter | solution.py:122
  268.3 5.7 copy-start.6
  273.9 1.6 copy-start.4
  273.9 1.8 copy-start.15
  273.9 3.0 copy-start.43
  275.5 1.0 copy-start.17
  280.5 22.9 %reduce-scatter.11.cloned.1.call-start = ((), (), s32[]{:S(2)}) async-start(), calls=%async_computation.14 | async-start | bytes 2359296 | tf_op jit(solution)/shard_map/reduce_scatter | solution.py:109
  289.9 1.5 copy-start.3
  290.0 30.0 %all-gather.17.cloned.1.call-start = ((), (), s32[]{:S(2)}) async-start(), calls=%async_computation.17 | async-start | bytes 2359296 | tf_op jit(solution)/shard_map/all_gather | solution.py:101
  291.4 12.0 %copy-start.10 = (bf16[512,768]{1,0:T(8,128)(2,1)S(1)}, bf16[512,768]{1,0:T(8,128)(2,1)}, u32[]{:S(2)}) copy-start(bf16[512,768]{1,0:T(8,128)(2,1)} %reduce-scatter.13.cloned.1.call-done) | copy-start | bytes 2359300
  303.4 4.3 copy-start.7
  306.5 1.2 copy-start.8
  306.5 1.2 copy-start.36
  307.7 1.6 copy-start.16
  308.8 153.7 %reduce-scatter.21.cloned.1.call-start = ((), (), s32[]{:S(2)}) async-start(), calls=%async_computation.21 | async-start | bytes 4177920 | tf_op jit(solution)/shard_map/reduce_scatter | solution.py:269
  315.1 4.9 copy-start.24
  315.2 158.6 %reduce-scatter.15.cloned.1.call-start = ((), (), s32[]{:S(2)}) async-start(), calls=%async_computation.18 | async-start | bytes 2359296 | tf_op jit(solution)/shard_map/reduce_scatter | solution.py:122
  323.3 5.0 copy-start.27
  417.8 3.5 copy-start.12
  417.8 3.5 copy-start.14
  428.4 5.8 copy-start.5
  434.2 5.9 copy-start.19
  434.2 172.1 %reduce-scatter.23.cloned.1.call-start = ((), (), s32[]{:S(2)}) async-start(), calls=%async_computation.22 | async-start | bytes 2088960 | tf_op jit(solution)/shard_map/reduce_scatter | solution.py:270
  440.0 3.8 copy-start.20
  440.0 3.8 copy-start.21
  440.0 3.8 copy-start.22
  440.0 294.9 %reduce-scatter.19.cloned.1.call-start = ((), (), s32[]{:S(2)}) async-start(), calls=%async_computation.20 | async-start | bytes 1253376 | tf_op jit(solution)/shard_map/reduce_scatter | solution.py:309
  443.7 430.1 %reduce-scatter.17.cloned.1.call-start = ((), (), s32[]{:S(2)}) async-start(), calls=%async_computation.19 | async-start | bytes 3760128 | tf_op jit(solution)/shard_map/reduce_scatter | solution.py:308
  449.2 24.5 %copy-start.1 = (f32[512,768]{1,0:T(8,128)S(1)}, f32[512,768]{1,0:T(8,128)}, u32[]{:S(2)}) copy-start(f32[512,768]{1,0:T(8,128)} %param.13) | copy-start | bytes 4718596
  449.2 24.5 %copy-start.30 = (f32[768]{0:T(1024)S(1)}, f32[768]{0:T(1024)}, u32[]{:S(2)}) copy-start(f32[768]{0:T(1024)} %copy-done.29) | copy-start | bytes 9220
  449.2 24.5 %copy-start.32 = (f32[512]{0:T(512)S(1)}, f32[512]{0:T(512)}, u32[]{:S(2)}) copy-start(f32[512]{0:T(512)} %copy-done.31) | copy-start | bytes 6148
  449.2 26.1 %copy-start.39 = (f32[512]{0:T(512)S(1)}, f32[512]{0:T(512)}, u32[]{:S(2)}) copy-start(f32[512]{0:T(512)} %copy-done.38) | copy-start | bytes 6148
  449.2 26.1 %copy-start.35 = (f32[512]{0:T(512)S(1)}, f32[512]{0:T(512)}, u32[]{:S(2)}) copy-start(f32[512]{0:T(512)} %copy-done.34) | copy-start | bytes 6148
  464.2 12.0 %copy-start.40 = (f32[768]{0:T(1024)S(1)}, f32[768]{0:T(1024)}, u32[]{:S(2)}) copy-start(f32[768]{0:T(1024)} %get-tuple-element.229) | copy-start | bytes 9220
  464.2 57.9 %copy-start.37 = (f32[512]{0:T(512)S(1)}, f32[512]{0:T(512)}, u32[]{:S(2)}) copy-start(f32[512]{0:T(512)} %copy-done.36) | copy-start | bytes 6148
  473.7 1.6 copy-start.9
Sparse Core Ops, SparseCore 0:
  56.0 5.6 all-gather.6
  64.4 60.1 all-gather.8
  161.3 7.8 reduce-scatter.8
  170.7 10.9 all-gather.14
  185.2 67.7 all-gather.12
  255.0 9.1 all-gather.10
  280.6 10.2 reduce-scatter.12
  293.1 10.2 reduce-scatter.10
  308.9 10.9 all-gather.16
  325.7 136.7 reduce-scatter.20
  465.4 8.2 reduce-scatter.14
  479.0 127.2 reduce-scatter.22
  612.3 122.5 reduce-scatter.18
  741.3 132.5 reduce-scatter.16
